TPU v7x, 128 devices: a whole 4x4x4 slice. The times are simulated.
128 devices in a mesh: dp: 8 (over z_hi, x), tensor: 16 (over z_lo, y, core).
Axes of the slice: x: 4, y: 4, z: 4 (z_hi: 2, z_lo: 2; z = z_hi * 2 + z_lo), core: 2. Of those that a mesh axis runs over, the one named last changes fastest.
Arguments:
- tokens: bfloat16 [5120, 4096], P('dp'), may hold values from -6 to 6
- hidden_grad: bfloat16 [5120, 14336], P('dp', 'tensor'), may hold values from -3 to 3
- gate_codes: int32 [4096, 14336], P(('dp', 'tensor')), may hold values from 0 to 15
- up_codes: int32 [4096, 14336], P(('dp', 'tensor')), may hold values from 0 to 15
- gate_groups: int32 [128, 14336], P(('dp', 'tensor')), may hold values from 0 to 15
- up_groups: int32 [128, 14336], P(('dp', 'tensor')), may hold values from 0 to 15
- gate_table: float32 [16], replicated, may hold values from 0.0015 to 0.0075
- up_table: float32 [16], replicated, may hold values from 0.0015 to 0.0075
Outputs:
- input_grad: bfloat16 [5120, 4096], P('dp', 'tensor')
- gate_grad: bfloat16 [4096, 14336], P(('dp', 'tensor'))
- up_grad: bfloat16 [4096, 14336], P(('dp', 'tensor'))
All inputs are finite; a program needn't handle non-finite values.
Results may differ from a plain program's by a relative error of at most 0.022.
Values may be sent and summed in bfloat16 or wider, within the bound.
No kernel may reach another device: no remote copies, remote signals or barrier semaphores. Data moves between devices by JAX's collectives and lax.ppermute only.
A program may use at most 128 MiB of HBM per device.

v0:
```python
import jax
import jax.numpy as jnp
from jax import lax
from jax.sharding import PartitionSpec as P


def dequantize(code_words, group_index, scale_table):
    levels = scale_table.shape[0]
    match = group_index[None, :, :] == jnp.arange(levels, dtype=jnp.int32)[:, None, None]
    scale_rows = jnp.sum(jnp.where(match, scale_table[:, None, None], jnp.float32(0.0)), axis=0)
    group_count = group_index.shape[0]
    shaped = (code_words - 8).reshape(group_count, -1, code_words.shape[1]).astype(jnp.float32)
    return (shaped * scale_rows[:, None, :]).reshape(code_words.shape).astype(jnp.bfloat16)


def shards(tokens, hidden_grad, gate_codes, up_codes, gate_groups, up_groups, gate_table, up_table):
    data_count = lax.axis_size("dp")
    tensor_count = lax.axis_size("tensor")
    own_rows = gate_codes.shape[0]
    hidden_local = hidden_grad.shape[1]
    own_gate = dequantize(gate_codes, gate_groups, gate_table)
    own_up = dequantize(up_codes, up_groups, up_table)
    local_gate, local_up = (
        lax.all_to_all(own_gate, "tensor", split_axis=1, concat_axis=0, tiled=True),
        lax.all_to_all(own_up, "tensor", split_axis=1, concat_axis=0, tiled=True),
    )
    w_gate, w_up = (
        lax.all_gather(local_gate, "dp", axis=0, tiled=True),
        lax.all_gather(local_up, "dp", axis=0, tiled=True),
    )
    gate_pre = jnp.dot(tokens, w_gate, preferred_element_type=jnp.float32)
    up_pre = jnp.dot(tokens, w_up, preferred_element_type=jnp.float32)
    sigmoid_gate = jax.nn.sigmoid(gate_pre)
    upstream = hidden_grad.astype(jnp.float32)
    d_gate = (upstream * up_pre * sigmoid_gate * (1.0 + gate_pre * (1.0 - sigmoid_gate))).astype(
        jnp.bfloat16
    )
    d_up = (upstream * gate_pre * sigmoid_gate).astype(jnp.bfloat16)
    back_dims = (((1,), (1,)), ((), ()))
    partial_value = lax.dot_general(
        d_gate, w_gate, back_dims, preferred_element_type=jnp.float32
    ) + lax.dot_general(d_up, w_up, back_dims, preferred_element_type=jnp.float32)
    input_grad = lax.psum_scatter(
        partial_value.astype(jnp.bfloat16), "tensor", scatter_dimension=1, tiled=True
    )
    token_dims = (((0,), (0,)), ((), ()))
    devices_all = data_count * tensor_count
    part_gate = lax.dot_general(tokens, d_gate, token_dims, preferred_element_type=jnp.float32)
    part_up = lax.dot_general(tokens, d_up, token_dims, preferred_element_type=jnp.float32)
    part_gate = part_gate.astype(jnp.bfloat16).reshape(devices_all, own_rows, hidden_local)
    part_up = part_up.astype(jnp.bfloat16).reshape(devices_all, own_rows, hidden_local)
    received_gate, received_up = (
        lax.all_to_all(part_gate, ("dp", "tensor"), split_axis=0, concat_axis=0, tiled=True),
        lax.all_to_all(part_up, ("dp", "tensor"), split_axis=0, concat_axis=0, tiled=True),
    )

    def settle(received):
        summed = (
            received.reshape(data_count, tensor_count, own_rows, hidden_local)
            .astype(jnp.float32)
            .sum(axis=0)
        )
        return (
            jnp.transpose(summed, (1, 0, 2))
            .reshape(own_rows, tensor_count * hidden_local)
            .astype(jnp.bfloat16)
        )

    gate_grad = settle(received_gate)
    up_grad = settle(received_up)
    return (input_grad, gate_grad, up_grad)


def solution(mesh):
    placed = (
        P("dp", None),
        P("dp", "tensor"),
        P(("dp", "tensor"), None),
        P(("dp", "tensor"), None),
        P(("dp", "tensor"), None),
        P(("dp", "tensor"), None),
        P(),
        P(),
    )
    return jax.shard_map(
        shards,
        mesh=mesh,
        in_specs=placed,
        out_specs=(P("dp", "tensor"), P(("dp", "tensor"), None), P(("dp", "tensor"), None)),
        check_vma=False,
    )
```

profile of v0, /device:TPU:6, one launch (start us, length us, event | category | flops | bytes accessed | tf_op | source)
XLA Modules:
  0.0 504.4 jit_solution(16500890266862725104)
XLA Ops:
  7.2 0.0 all-gather.5.cloned.1.call-start
  7.2 1.1 select_reduce_fusion
  8.3 1.7 multiply_convert_fusion
  10.0 0.0 copy-start.2
  10.1 0.0 copy-start.3
  10.1 0.0 copy-start
  10.1 0.1 copy.45
  10.2 20.8 %all_to_all.42 = bf16[32,16,896]{2,0,1:T(8,128)(2,1)} all-to-all(bf16[32,16,896]{2,0,1:T(8,128)(2,1)S(1)} %bitcast.68), channel_id=1, replica_groups=mesh['dp'=8,'tensor'=16] {'tensor'}, dimensions={1} | all-to-all | bytes 1835008 | tf_op jit(solution)/shard_map/all_to_all | solution.py:24
  31.0 0.0 all-gather.5.cloned.1.call-update
  31.0 0.0 all-gather.3.cloned.1.call-start
  31.0 0.0 copy-done.2
  31.0 0.0 copy-done.3
  31.1 0.3 select_reduce_fusion.1
  31.3 0.0 copy-done
  31.3 0.2 multiply_convert_fusion.1
  31.6 0.0 copy-start.1
  31.6 0.1 copy.46
  31.6 18.3 %all_to_all.43 = bf16[32,16,896]{2,0,1:T(8,128)(2,1)} all-to-all(bf16[32,16,896]{2,0,1:T(8,128)(2,1)S(1)} %bitcast.69), channel_id=1, replica_groups=mesh['dp'=8,'tensor'=16] {'tensor'}, dimensions={1} | all-to-all | bytes 1835008 | tf_op jit(solution)/shard_map/all_to_all | solution.py:25
  49.9 0.0 all-gather.3.cloned.1.call-update
  49.9 0.0 copy-done.1
  49.9 1.1 copy.32
  51.1 81.3 %all-gather.5.cloned.1.call-done = bf16[4096,896]{1,0:T(8,128)(2,1)} async-done(((bf16[512,896]{1,0:T(8,128)(2,1)}), bf16[4096,896]{1,0:T(8,128)(2,1)}) %all-gather.5.cloned.1.call-update) | async-done | bytes 7340048 | tf_op jit(solution)/shard_map/all_gather | solution.py:28
  132.4 9.0 %fusion.11 = f32[896,640]{1,0:T(8,128)S(1)} fusion(bf16[4096,896]{1,0:T(8,128)(2,1)} %all-gather.5.cloned.1.call-done, bf16[640,4096]{1,0:T(8,128)(2,1)} %param.8), kind=kOutput, calls=%fused_computation.24 | convolution fusion | flops 4697620480 | bytes 14876672 | tf_op jit(solution)/shard_map/dot_general | solution.py:31
  141.4 0.0 copy-start.4
  141.4 1.4 copy-done.4
  142.8 11.0 %convert_bitcast_fusion = bf16[4096,896]{0,1:T(8,128)(2,1)} fusion(bf16[640,4096]{1,0:T(8,128)(2,1)} %param.8, bf16[640,896]{0,1:T(8,128)(2,1)S(1)} %copy.32, f32[896,640]{1,0:T(8,128)S(1)} %fusion.11), kind=kOutput, calls=%fused_computation.1 | convolution fusion | flops 4705304576 | bytes 16023552 | tf_op jit(solution)/shard_map/dot_general | solution.py:49
  153.8 10.9 %copy.37 = bf16[4096,896]{1,0:T(8,128)(2,1)} copy(bf16[4096,896]{0,1:T(8,128)(2,1)} %convert_bitcast_fusion) | data formatting | bytes 14680064 | tf_op jit(solution)/shard_map/convert_element_type | solution.py:51
  164.6 7.6 %all-to-all-start.3 = ((bf16[128,32,896]{2,1,0:T(8,128)(2,1)}), bf16[128,32,896]{2,1,0:T(8,128)(2,1)}, u32[]{:S(2)}, u32[]{:S(2)}) async-start(bf16[128,32,896]{2,1,0:T(8,128)(2,1)} %bitcast.62), calls=%async_computation.4 | async-start | bytes 14680064 | tf_op jit(solution)/shard_map/all_to_all | solution.py:54
  172.3 0.2 reduce-scatter.2.cloned.1.call-start
  172.5 143.8 %all-gather.3.cloned.1.call-done = bf16[4096,896]{1,0:T(8,128)(2,1)} async-done(((bf16[512,896]{1,0:T(8,128)(2,1)}), bf16[4096,896]{1,0:T(8,128)(2,1)}) %all-gather.3.cloned.1.call-update) | async-done | bytes 7340048 | tf_op jit(solution)/shard_map/all_gather | solution.py:29
  316.3 11.6 %fusion.2 = bf16[640,896]{0,1:T(8,128)(2,1)S(1)} fusion(bf16[640,896]{0,1:T(8,128)(2,1)S(1)} %copy.32, f32[896,640]{1,0:T(8,128)} %copy-done.4, bf16[4096,896]{1,0:T(8,128)(2,1)} %all-gather.3.cloned.1.call-done, bf16[640,4096]{1,0:T(8,128)(2,1)} %param.8), kind=kOutput, calls=%fused_computation.7 | convolution fusion | flops 4703928320 | bytes 17170432 | tf_op jit(solution)/shard_map/dot_general | solution.py:32
  327.9 0.0 slice-start.1
  327.9 0.0 copy-start.5
  327.9 10.6 %fusion.12 = f32[640,4096]{1,0:T(8,128)} fusion(bf16[640,896]{0,1:T(8,128)(2,1)S(1)} %fusion.2, bf16[4096,896]{1,0:T(8,128)(2,1)} %all-gather.5.cloned.1.call-done), kind=kOutput, calls=%fused_computation.25 | convolution fusion | flops 4697620480 | bytes 18972672 | tf_op jit(solution)/shard_map/dot_general | solution.py:40
  338.5 0.0 slice-done
  338.5 0.0 slice-done.1
  338.5 10.2 %add_convert_fusion = bf16[640,4096]{1,0:T(8,128)(2,1)} fusion(f32[640,4096]{1,0:T(8,128)} %fusion.12, bf16[4096,896]{1,0:T(8,128)(2,1)S(1)} %bitcast.77, bf16[640,896]{0,1:T(8,128)(2,1)S(1)} %copy.32, f32[896,640]{1,0:T(8,128)S(1)} %copy-done.5), kind=kOutput, calls=%fused_computation | convolution fusion | flops 4706877440 | bytes 26509312 | tf_op jit(solution)/shard_map/dot_general | solution.py:42
  348.7 0.0 reduce-scatter.2.cloned.1.call-update
  348.7 10.4 %convert_bitcast_fusion.1 = bf16[4096,896]{0,1:T(8,128)(2,1)} fusion(bf16[640,896]{0,1:T(8,128)(2,1)S(1)} %fusion.2, bf16[640,4096]{1,0:T(8,128)(2,1)} %param.8), kind=kOutput, calls=%fused_computation.2 | convolution fusion | flops 4701290496 | bytes 13729792 | tf_op jit(solution)/shard_map/dot_general | solution.py:48
  359.1 10.8 %copy.35 = bf16[4096,896]{1,0:T(8,128)(2,1)} copy(bf16[4096,896]{0,1:T(8,128)(2,1)} %convert_bitcast_fusion.1) | data formatting | bytes 14680064 | tf_op jit(solution)/shard_map/convert_element_type | solution.py:50
  370.0 0.0 all-to-all-done.3
  370.0 9.5 %all-to-all-start.2 = ((bf16[128,32,896]{2,1,0:T(8,128)(2,1)}), bf16[128,32,896]{2,1,0:T(8,128)(2,1)}, u32[]{:S(2)}, u32[]{:S(2)}) async-start(bf16[128,32,896]{2,1,0:T(8,128)(2,1)} %bitcast.63), calls=%async_computation.3 | async-start | bytes 14680064 | tf_op jit(solution)/shard_map/all_to_all | solution.py:53
  379.4 4.6 reduce.3
  384.0 1.0 copy.42
  385.0 92.1 %all-to-all-done.2 = bf16[128,32,896]{2,1,0:T(8,128)(2,1)} async-done(((bf16[128,32,896]{2,1,0:T(8,128)(2,1)}), bf16[128,32,896]{2,1,0:T(8,128)(2,1)}, u32[]{:S(2)}, u32[]{:S(2)}) %all-to-all-start.2) | async-done | bytes 7340064 | tf_op jit(solution)/shard_map/all_to_all | solution.py:53
  477.2 4.5 reduce.2
  481.7 1.0 copy.41
  482.7 15.2 %reduce-scatter.2.cloned.1.call-done = bf16[640,256]{1,0:T(8,128)(2,1)} async-done(((bf16[640,4096]{1,0:T(8,128)(2,1)}), bf16[640,256]{1,0:T(8,128)(2,1)}) %reduce-scatter.2.cloned.1.call-update) | async-done | bytes 327696 | tf_op jit(solution)/shard_map/reduce_scatter | solution.py:43
  (3 shorter events, 0.0 us)
Async XLA Ops:
  7.2 125.2 %all-gather.5.cloned.1.call-start = ((), (), s32[]{:S(2)}) async-start(), calls=%async_computation.6 | async-start | bytes 8257536 | tf_op jit(solution)/shard_map/all_gather | solution.py:28
  10.0 21.0 %copy-start.2 = (s32[1,14336]{1,0:T(1,128)S(1)}, s32[1,14336]{1,0:T(1,128)}, u32[]{:S(2)}) copy-start(s32[1,14336]{1,0:T(1,128)} %param.13) | copy-start | bytes 172036
  10.1 21.0 %copy-start.3 = (f32[16]{0:T(128)S(1)}, f32[16]{0:T(128)}, u32[]{:S(2)}) copy-start(f32[16]{0:T(128)} %param.15) | copy-start | bytes 196
  10.1 21.2 %copy-start = (s32[32,14336]{1,0:T(8,128)S(1)}, s32[32,14336]{1,0:T(8,128)}, u32[]{:S(2)}) copy-start(s32[32,14336]{1,0:T(8,128)} %param.11) | copy-start | bytes 5505028
  31.0 285.3 %all-gather.3.cloned.1.call-start = ((), (), s32[]{:S(2)}) async-start(), calls=%async_computation.5 | async-start | bytes 8257536 | tf_op jit(solution)/shard_map/all_gather | solution.py:29
  31.6 18.4 %copy-start.1 = (bf16[640,896]{1,0:T(8,128)(2,1)S(1)}, bf16[640,896]{1,0:T(8,128)(2,1)}, u32[]{:S(2)}) copy-start(bf16[640,896]{1,0:T(8,128)(2,1)} %param.9) | copy-start | bytes 3440644
  141.4 1.4 copy-start.4
  164.6 205.3 %all-to-all-start.3 = ((bf16[128,32,896]{2,1,0:T(8,128)(2,1)}), bf16[128,32,896]{2,1,0:T(8,128)(2,1)}, u32[]{:S(2)}, u32[]{:S(2)}) async-start(bf16[128,32,896]{2,1,0:T(8,128)(2,1)} %bitcast.62), calls=%async_computation.4 | async-start | bytes 14680064 | tf_op jit(solution)/shard_map/all_to_all | solution.py:54
  172.3 325.6 %reduce-scatter.2.cloned.1.call-start = ((), (), s32[]{:S(2)}) async-start(), calls=%async_computation.7 | async-start | bytes 5570560 | tf_op jit(solution)/shard_map/reduce_scatter | solution.py:43
  316.3 22.3 %slice-start = ((s8[7340032]{0:T(1024)(128)(4,1)}), s8[4194304]{0:T(1024)(128)(4,1)S(1)}, s32[]{:S(2)}) async-start(s8[7340032]{0:T(1024)(128)(4,1)} %bitcast.76), calls=%async_computation.8 | async-start | bytes 8388608
  327.9 10.7 %slice-start.1 = ((s8[7340032]{0:T(1024)(128)(4,1)}), s8[3145728]{0:T(1024)(128)(4,1)S(1)}, s32[]{:S(2)}) async-start(s8[7340032]{0:T(1024)(128)(4,1)} %bitcast.76), calls=%async_computation.9 | async-start | bytes 6291456
  327.9 10.6 %copy-start.5 = (f32[896,640]{1,0:T(8,128)S(1)}, f32[896,640]{1,0:T(8,128)}, u32[]{:S(2)}) copy-start(f32[896,640]{1,0:T(8,128)} %copy-done.4) | copy-start | bytes 6881284
  370.0 107.2 %all-to-all-start.2 = ((bf16[128,32,896]{2,1,0:T(8,128)(2,1)}), bf16[128,32,896]{2,1,0:T(8,128)(2,1)}, u32[]{:S(2)}, u32[]{:S(2)}) async-start(bf16[128,32,896]{2,1,0:T(8,128)(2,1)} %bitcast.63), calls=%async_computation.3 | async-start | bytes 14680064 | tf_op jit(solution)/shard_map/all_to_all | solution.py:53
Sparse Core Ops, SparseCore 0:
  31.1 101.2 all-gather.4
  134.7 181.5 all-gather.2
  348.9 148.9 reduce-scatter.1
where the time goes:
time: 505 us; the launch traced here: 504 us
  waiting for transfers between devices  332 us (66%)
  matrix products  62.8 us (12%)
  blocking collectives  39.1 us (8%)
  local copies, waits for them, and re-layouts  26.4 us (5%)
  starting transfers between devices  17.4 us (3%)
  between operations  13.9 us (3%)
  other arithmetic  12.4 us (2%)
    all_gather x1, waiting for transfers between devices, shards(): lax.all_gather(local_up, 'dp', axis=0, tiled=True)  144 us
    all_to_all x1, waiting for transfers between devices, shards(): lax.all_to_all(part_gate, ('dp', 'tensor'), split_axis=0, concat_axis=0,...  92.1 us
    all_gather x1, waiting for transfers between devices, shards(): lax.all_gather(local_gate, 'dp', axis=0, tiled=True)  81.3 us
    all_to_all x1, blocking collectives, shards(): lax.all_to_all(own_gate, 'tensor', split_axis=1, concat_axis=0, tiled=True)  20.8 us
    all_to_all x1, blocking collectives, shards(): lax.all_to_all(own_up, 'tensor', split_axis=1, concat_axis=0, tiled=True)  18.3 us
    reduce_scatter x1, waiting for transfers between devices, shards(): lax.psum_scatter(partial_value.astype(jnp.bfloat16), 'tensor', scatter_di...  15.2 us
    dot_general x1, matrix products, shards(): up_pre = jnp.dot(tokens, w_up, preferred_element_type=jnp.float32)  11.6 us
    dot_general x1, matrix products, shards(): lax.dot_general(tokens, d_up, token_dims, preferred_element_type=jnp.floa...  11 us
  transfers between devices with their start and end apart: 5, of which 4 were waited for; matrix products, arithmetic and copies ran while one was open for 19% of the time, Pallas kernels for 0%

commit v1 on v0

v1 whole, which is shorter than its diff:
```python
import jax
import jax.numpy as jnp
from jax import lax
from jax.experimental import pallas as pl
from jax.experimental.pallas import tpu as pltpu
from jax.sharding import Mesh
from jax.sharding import PartitionSpec as P

F32 = jnp.float32
BF16 = jnp.bfloat16
SLABS = 8
HIDDEN = ("zh", "zl", "y", "c")
VMEM_LIMIT = 26 * 1024 * 1024


def params():
    return pltpu.CompilerParams(vmem_limit_bytes=VMEM_LIMIT)


HEAVY = 65536


def cost(flops, nbytes):
    return pl.CostEstimate(flops=flops // 64, bytes_accessed=nbytes // 64, transcendentals=0)


def shape(*dims, kind=BF16):
    return jax.ShapeDtypeStruct(dims, kind)


def after(value, *others):
    return lax.optimization_barrier((value, *others))[0]


def dot(a, b, dims=((1,), (0,))):
    return lax.dot_general(a, b, (dims, ((), ())), preferred_element_type=F32)


def dequantized(codes, groups, tables, halves, outer):
    rows, width = codes[0].shape
    part = width // (halves * outer)
    pair = halves * part
    per = 4
    levels = tables[0].shape[0]

    def body(gate_table, up_table, gate_codes, up_codes, gate_groups, up_groups, o_ref):
        both = ((gate_table, gate_codes, gate_groups), (up_table, up_codes, up_groups))
        for b in range(per):
            at = pl.ds(b * pair, pair)
            for w, (table, c_ref, g_ref) in enumerate(both):
                index = g_ref[:, at]
                scale = jnp.full(index.shape, table[0], F32)
                for k in range(1, levels):
                    scale = jnp.where(index == k, table[k], scale)
                value = ((c_ref[:, at] - 8).astype(F32) * scale).astype(BF16)
                for h in range(halves):
                    o_ref[h, b, :, w * part : (w + 1) * part] = value[:, h * part : (h + 1) * part]

    table_spec = pl.BlockSpec(memory_space=pltpu.SMEM)
    code_spec = pl.BlockSpec((rows, per * pair), lambda i: (0, i))
    group_spec = pl.BlockSpec((1, per * pair), lambda i: (0, i))
    return pl.pallas_call(
        body,
        out_shape=shape(halves, outer, rows, 2 * part),
        grid=(outer // per,),
        in_specs=[table_spec, table_spec, code_spec, code_spec, group_spec, group_spec],
        out_specs=pl.BlockSpec((halves, per, rows, 2 * part), lambda i: (0, i, 0, 0)),
        compiler_params=params(),
        cost_estimate=cost(0, 12 * rows * width),
    )(*tables, *codes, *groups)


def gathered_columns(blocks):
    halves, outer, rows, both = blocks.shape
    part = both // 2
    pair = halves * part
    per = 4

    def body(b_ref, gate_ref, up_ref):
        for b in range(per):
            for h in range(halves):
                at = pl.ds(b * pair + h * part, part)
                gate_ref[:, at] = b_ref[h, b, :, :part]
                up_ref[:, at] = b_ref[h, b, :, part:]

    out = shape(rows, outer * pair)
    out_spec = pl.BlockSpec((rows, per * pair), lambda i: (0, i))
    return pl.pallas_call(
        body,
        out_shape=(out, out),
        grid=(outer // per,),
        in_specs=[pl.BlockSpec((halves, per, rows, both), lambda i: (0, i, 0, 0))],
        out_specs=(out_spec, out_spec),
        compiler_params=params(),
        cost_estimate=cost(0, 8 * halves * outer * rows * both // 2),
    )(blocks)


def ordered_tokens(slabs, tokens, width, half, into=None):
    rows = tokens.shape[0]
    count = slabs.shape[0]
    more = [] if into is None else [into]

    def body(slabs_ref, t_ref, *rest):
        rest[-1][0] = t_ref[...]

    return pl.pallas_call(
        body,
        out_shape=shape(count, 2 * rows, width),
        grid_spec=pltpu.PrefetchScalarGridSpec(
            num_scalar_prefetch=1,
            grid=(count,),
            in_specs=[pl.BlockSpec((rows, width), lambda i, s: (0, s[i]))]
            + [pl.BlockSpec(memory_space=pl.ANY)] * len(more),
            out_specs=pl.BlockSpec((1, rows, width), lambda i, s: (i, half, 0)),
        ),
        input_output_aliases={2: 0} if more else {},
        compiler_params=params(),
        cost_estimate=cost(0, 4 * rows * width * count),
    )(slabs, tokens, *more)


def products(t_ref, weights):
    total = None
    for j, w_ref in enumerate(weights):
        term = dot(t_ref[j], w_ref[...])
        total = term if total is None else total + term
    return total


TILE = 320


def forward_first(tokens, weights):
    width, both = weights[0].shape
    count, rows = len(weights), tokens.shape[1]

    def body(t_ref, *rest):
        rest[-1][...] = products(t_ref, rest[:-1])

    return pl.pallas_call(
        body,
        out_shape=shape(rows, both, kind=F32),
        grid=(rows // TILE,),
        in_specs=[pl.BlockSpec((count, TILE, width), lambda i: (0, i, 0))]
        + [pl.BlockSpec((width, both), lambda i: (0, 0))] * count,
        out_specs=pl.BlockSpec((TILE, both), lambda i: (i, 0)),
        compiler_params=params(),
        cost_estimate=cost(2 * count * rows * width * both, 2 * count * rows * width + 4 * rows * both),
    )(tokens, *weights)


def forward_last(tokens, weights, acc, grad_own, grad_other):
    width, both = weights[0].shape
    part = both // 2
    slabs, rows, _ = tokens.shape
    tiles = rows // TILE // 2

    def body(t_ref, low, high, acc_ref, ga_ref, gb_ref, o_ref):
        pre = acc_ref[...] + products(t_ref, (low, high))
        gate, up = pre[:, :part], pre[:, part:]
        s = jax.nn.sigmoid(gate)
        g = jnp.where(pl.program_id(0) < tiles, ga_ref[...].astype(F32), gb_ref[:, :part].astype(F32))
        o_ref[:, :part] = (g * up * s * (1.0 + gate * (1.0 - s))).astype(BF16)
        o_ref[:, part:] = (g * gate * s).astype(BF16)

    slab = pl.BlockSpec((width, both), lambda i: (0, 0))
    tall = pl.BlockSpec((TILE, both), lambda i: (i, 0))
    return pl.pallas_call(
        body,
        out_shape=shape(rows, both),
        grid=(rows // TILE,),
        in_specs=[
            pl.BlockSpec((2, TILE, width), lambda i: (slabs // 2 - 1, i, 0)),
            slab,
            slab,
            tall,
            pl.BlockSpec((TILE, part), lambda i: (jnp.minimum(i, tiles - 1), 0)),
            pl.BlockSpec((TILE, grad_other.shape[1]), lambda i: (jnp.maximum(i - tiles, 0), 0)),
        ],
        out_specs=tall,
        compiler_params=params(),
        cost_estimate=cost(4 * rows * width * both, 4 * rows * width + 8 * rows * both),
    )(tokens, *weights, acc, grad_own, grad_other)


def weight_part(at, tokens, delta, adds, joined=False, heavy=1):
    count = len(at)
    _, rows, width = tokens.shape
    both = delta.shape[1]
    first, step = at[0], at[1] - at[0]
    flat = [a for some in adds for a in some]
    lengths = [len(some) for some in adds]

    def body(t_ref, d_ref, *rest):
        ins, outs = rest[: len(flat)], rest[len(flat) :]
        begin = 0
        for j in range(count):
            mine = ins[begin : begin + lengths[j]]
            begin += lengths[j]

            @pl.when(pl.program_id(0) == j)
            def _(j=j, mine=mine):
                total = dot(t_ref[0], d_ref[...], ((0,), (0,)))
                for a in mine:
                    total = total + a[...].astype(F32)
                o_ref = outs[0 if joined else j]
                o_ref[...] = total.astype(o_ref.dtype)

    slab = pl.BlockSpec((width, both), lambda i: (0, 0))
    if joined:
        out_shape, out_specs = shape(count * width, both, kind=F32), pl.BlockSpec((width, both), lambda i: (i, 0))
    else:
        out_shape, out_specs = (shape(width, both),) * count, (slab,) * count
    return pl.pallas_call(
        body,
        out_shape=out_shape,
        grid=(count,),
        in_specs=[
            pl.BlockSpec((1, rows, width), lambda i: (first + step * i, 0, 0)),
            pl.BlockSpec((rows, both), lambda i: (0, 0)),
        ]
        + [slab] * len(flat),
        out_specs=out_specs,
        compiler_params=params(),
        cost_estimate=cost(heavy * 2 * both * rows * width * count, 2 * rows * (width * count + both) + 2 * both * width * (count + len(flat))),
    )(tokens, delta, *flat)


def finished(total, low, high):
    width, both = low.shape
    tiles = 2

    def body(t_ref, l_ref, h_ref, o_ref):
        last = jnp.where(pl.program_id(0) < tiles, l_ref[...].astype(F32), h_ref[...].astype(F32))
        o_ref[...] = (t_ref[...] + last).astype(BF16)

    tile = width // tiles
    block = pl.BlockSpec((tile, both), lambda i: (i, 0))
    return pl.pallas_call(
        body,
        out_shape=shape(2 * width, both),
        grid=(2 * tiles,),
        in_specs=[
            block,
            pl.BlockSpec((tile, both), lambda i: (jnp.minimum(i, tiles - 1), 0)),
            pl.BlockSpec((tile, both), lambda i: (jnp.maximum(i - tiles, 0), 0)),
        ],
        out_specs=block,
        compiler_params=params(),
        cost_estimate=cost(0, 16 * width * both),
    )(total, low, high)


def input_part(where, delta, weights, add):
    tokens, both = delta.shape
    half = tokens // 2
    count = len(weights) // 2
    feats = weights[0].shape[0] // 2
    more = [] if add is None else [add]

    def body(where_ref, d_ref, *rest):
        o_ref = rest[-1]
        flip = where_ref[count]
        for j in range(count):

            @pl.when(pl.program_id(0) == j)
            def _(j=j):
                pair = jnp.concatenate([rest[2 * j][...], rest[2 * j + 1][...]], axis=0)
                total = dot(d_ref[...], pair, ((1,), (1,)))
                for h in range(2):
                    place = h + flip - 2 * h * flip
                    for z in range(2):
                        value = total[h * half : (h + 1) * half, z * feats : (z + 1) * feats]
                        if more:
                            value = value + rest[2 * count][place, z, 0].astype(F32)
                        o_ref[place, z, 0] = value.astype(BF16)

    o_spec = pl.BlockSpec((2, 2, 1, half, feats), lambda i, s: (0, 0, s[i], 0, 0))
    w_spec = pl.BlockSpec((feats, both), lambda i, s: (s[count + 1], 0))
    return pl.pallas_call(
        body,
        out_shape=shape(2, 2, count, half, feats),
        grid_spec=pltpu.PrefetchScalarGridSpec(
            num_scalar_prefetch=1,
            grid=(count,),
            in_specs=[pl.BlockSpec((tokens, both), lambda i, s: (0, 0))] + [w_spec] * (2 * count) + [o_spec] * len(more),
            out_specs=o_spec,
        ),
        compiler_params=params(),
        cost_estimate=cost(4 * tokens * both * feats * count, 4 * count * both * feats + 8 * tokens * feats * count),
    )(where, delta, *weights, *more)


def shards(tokens, hidden_grad, gate_codes, up_codes, gate_groups, up_groups, gate_table, up_table):
    zh, x, zl = lax.axis_index("zh"), lax.axis_index("x"), lax.axis_index("zl")
    y, core = lax.axis_index("y"), lax.axis_index("c")
    ring = lax.axis_size("x")
    halves, planes, cores = lax.axis_size("zh"), lax.axis_size("zl"), lax.axis_size("c")
    columns = lax.axis_size("y")
    outer = planes * columns * cores
    own_tokens, width_all = tokens.shape
    rows = gate_codes.shape[0]
    slab = width_all // (halves * ring)
    part = hidden_grad.shape[1] // halves
    right = [(i, (i + 1) % ring) for i in range(ring)]
    left = [(i, (i + ring - 1) % ring) for i in range(ring)]
    swap = [(0, 1), (1, 0)]
    crossed = [(i, halves * planes - 1 - i) for i in range(halves * planes)]

    def to_right(a):
        return lax.ppermute(a, "x", right)

    def to_left(a):
        return lax.ppermute(a, "x", left)

    def exchange(blocks):
        return lax.all_to_all(blocks.reshape(halves * outer, rows, 2 * part), HIDDEN, 0, 0, tiled=True)

    blocks = dequantized((gate_codes, up_codes), (gate_groups, up_groups), (gate_table, up_table), halves, outer)
    piece = own_tokens // outer
    mine = after(tokens, blocks)
    mine = lax.dynamic_slice_in_dim(mine, (((1 - zl) * columns + y) * cores + core) * piece, piece, 0)
    mine = lax.ppermute(mine, ("zh", "zl"), crossed)

    got = after(exchange(blocks), mine).reshape(halves, slab, 2 * part)
    low, high = got[0], got[1]
    other = lax.all_gather(after(mine, low), ("zl", "y", "c"), axis=0, tiled=True)
    from_left_low, from_right_high = to_right(low), to_left(high)
    from_left_high, from_right_low = to_right(high), to_left(low)
    far_low, far_high = to_right(from_left_low), to_left(from_right_high)
    near_weights = [low, high, from_right_low, from_right_high, from_left_low, from_left_high]
    far_weights = [far_low, far_high]

    xs = jnp.stack([x, (x + 1) % ring, (x + ring - 1) % ring, (x + 2) % ring]).astype(jnp.int32)
    order = (xs[:, None] + jnp.arange(halves, dtype=jnp.int32)[None, :] * ring).reshape(-1)
    every = ordered_tokens(order, after(tokens, low), slab, 0)
    grads = after(hidden_grad, every)
    first, second = grads[:, :part], grads[:, part:]
    grad_own = jnp.where(zh == 0, first, second)
    lanes = -(-part // 128) * 128
    grad_other = jnp.pad(jnp.where(zh == 0, second, first), ((0, 0), (0, lanes - part)))
    other = after(other, grad_other)
    every = ordered_tokens(order, other, slab, 1, every)
    grad_other = lax.ppermute(after(grad_other, other), "zh", swap)
    acc = forward_first(every, near_weights)
    delta = forward_last(every, far_weights, acc, grad_own, grad_other)

    def input_of(where_core, delta, add):
        where = jnp.concatenate([xs, jnp.stack([zh, where_core]).astype(jnp.int32)])
        return input_part(where, delta, near_weights + far_weights, add)

    none = ((), ())
    sum_low, sum_high = weight_part((6, 7), every, delta, none)
    got_low, got_high = to_right(sum_low), to_left(sum_high)
    away = input_of(1 - core, after(delta, sum_low), None)
    from_core = lax.ppermute(away, "c", swap)
    high_p, low_m = weight_part((3, 4), every, after(delta, away), none, heavy=HEAVY)
    one_low, one_high = to_left(low_m), to_right(high_p)
    here = input_of(core, after(delta, low_m), from_core)
    input_grad = lax.psum_scatter(here.reshape(-1, here.shape[4]), ("zh", "zl", "y"), scatter_dimension=0, tiled=True)
    low_p, high_m = weight_part((2, 5), every, after(delta, here), ((got_low,), (got_high,)), heavy=HEAVY)
    two_low, two_high = to_right(low_p), to_left(high_m)
    total = weight_part((0, 1), every, after(delta, low_p), ((one_low,), (one_high,)), True)
    summed = finished(total, two_low, two_high)
    gate_grad, up_grad = gathered_columns(exchange(summed).reshape(halves, outer, rows, 2 * part))
    return input_grad, gate_grad, up_grad


def solution(mesh):
    fine = Mesh(mesh.devices.reshape(2, 4, 2, 4, 2), ("zh", "x", "zl", "y", "c"))
    data, hidden = ("zh", "x"), ("zl", "y", "c")
    rows = P(data + hidden, None)
    return jax.shard_map(
        shards,
        mesh=fine,
        in_specs=(P(data, None), P(data, hidden), rows, rows, rows, rows, P(), P()),
        out_specs=(P(data, hidden), rows, rows),
        check_vma=False,
    )
```

time: 505 us -> 267 us (0.53)
  waiting for transfers between devices: 332 us -> 88.4 us
  matrix products: 62.8 us -> 0 us
  Pallas kernels: 0 us -> 62.7 us
  local copies, waits for them, and re-layouts: 26.4 us -> 39.2 us
  starting transfers between devices: 17.4 us -> 29.2 us
  other arithmetic: 12.4 us -> 1.26 us
  blocking collectives: 39.1 us -> 30.6 us
    all_gather x2 -> x1, waiting for transfers between devices: 225 us -> 10.8 us  [shards(): lax.all_gather(after(mine, low), ('zl', 'y', 'c'), axis=0, tiled=True)]
    all_to_all x2 -> x1, waiting for transfers between devices: 92.1 us -> 0.01 us  [exchange(): lax.all_to_all(blocks.reshape(halves * outer, rows, 2 * part), HIDDEN, 0,...]
    ppermute x0 -> x15, waiting for transfers between devices: none -> 63.5 us  [the longest x1 26.6 us: shards(): mine = lax.ppermute(mine, ('zh', 'zl'), crossed)]
    dot_general x6 -> x0, matrix products: 62.8 us -> none  [the longest x1 11.6 us: shards(): up_pre = jnp.dot(tokens, w_up, preferred_element_type=jnp.float32)]
    pallas_call x0 -> x13, Pallas kernels: none -> 62.7 us  [the longest x2 19.1 us: input_part(): pl.pallas_call(body, out_shape=shape(2, 2, count, half, feats), grid_spec...]
    unnamed x17 -> x52, local copies, waits for them, and re-layouts: 2.57 us -> 35.3 us
    convert_element_type x6 -> x0, local copies, waits for them, and re-layouts: 23.8 us -> none  [the longest x1 10.9 us: shards(): part_up.astype(jnp.bfloat16).reshape(devices_all, own_rows, hidden_local)]
    ppermute x0 -> x15, starting transfers between devices: none -> 20.6 us  [the longest x6 7.82 us: to_right(): return lax.ppermute(a, 'x', right)]
  transfers between devices with their start and end apart: 5 -> 18, of which waited for: 4 -> 9; matrix products, arithmetic and copies ran while one was open for 19% -> 1% of each run, Pallas kernels for 0% -> 15%
where the time goes in v1:
time: 267 us; the launch traced here: 266 us
  waiting for transfers between devices  88.4 us (33%)
  Pallas kernels  62.7 us (23%)
  local copies, waits for them, and re-layouts  39.2 us (15%)
  blocking collectives  30.6 us (11%)
  starting transfers between devices  29.2 us (11%)
  between operations  14.3 us (5%)
    unnamed x52, local copies, waits for them, and re-layouts  35.3 us
    all_to_all x1, blocking collectives, exchange(): lax.all_to_all(blocks.reshape(halves * outer, rows, 2 * part), HIDDEN, 0,...  30.6 us
    ppermute x1, waiting for transfers between devices, shards(): mine = lax.ppermute(mine, ('zh', 'zl'), crossed)  26.6 us
    ppermute x6, waiting for transfers between devices, to_right(): return lax.ppermute(a, 'x', right)  22.6 us
    pallas_call x2, Pallas kernels, input_part(): pl.pallas_call(body, out_shape=shape(2, 2, count, half, feats), grid_spec...  19.1 us
    pallas_call x4, Pallas kernels, weight_part(): pl.pallas_call(body, out_shape=out_shape, grid=(count,), in_specs=[pl.Blo...  17.9 us
    ppermute x6, waiting for transfers between devices, to_left(): return lax.ppermute(a, 'x', left)  14.3 us
    reduce_scatter x1, waiting for transfers between devices, shards(): lax.psum_scatter(here.reshape(-1, here.shape[4]), ('zh', 'zl', 'y'), scat...  14 us
  transfers between devices with their start and end apart: 18, of which 9 were waited for; matrix products, arithmetic and copies ran while one was open for 1% of the time, Pallas kernels for 15%

profile of v1, /device:TPU:6, one launch (start us, length us, event | category | flops | bytes accessed | tf_op | source)
XLA Modules:
  0.0 265.6 jit_solution(6897983169764531062)
XLA Ops:
  7.2 1.5 copy-done.13
  8.7 1.5 copy-done.14
  13.1 3.0 %shard_map.103 = bf16[2,16,32,896]{3,2,1,0:T(8,128)(2,1)} custom-call(f32[16]{0:T(128)S(1)} %copy-done.19, f32[16]{0:T(128)S(1)} %copy-done.20, s32[32,14336]{1,0:T(8,128)S(1)} %copy-done.13, s32[32,14336]{1,0:T(8,128)S(1)} %copy-done.14, s32[1,14336]{1,0:T(1,128)S(1)} %copy-done.17, s32[1,14336]{1,0:T(1,128)S(1)} %copy-done.18), custom_call_target="tpu_custom_call" | custom-call | bytes 86016 | tf_op jit(solution)/shard_map/pallas_call | solution.py:62
  16.1 8.4 %all-to-all-start = ((bf16[32,32,896]{2,1,0:T(8,128)(2,1)}), bf16[32,32,896]{2,1,0:T(8,128)(2,1)}, u32[]{:S(2)}, u32[]{:S(2)}) async-start(bf16[32,32,896]{2,1,0:T(8,128)(2,1)} %bitcast.6), calls=%async_computation | async-start | bytes 3670016 | tf_op jit(solution)/shard_map/all_to_all | solution.py:318
  24.6 1.0 constant_dynamic-slice_fusion
  25.6 3.1 %collective-permute-start = (bf16[40,4096]{1,0:T(8,128)(2,1)S(1)}, bf16[40,4096]{1,0:T(8,128)(2,1)S(1)}, u32[]{:S(2)}, u32[]{:S(2)}) collective-permute-start(bf16[40,4096]{1,0:T(8,128)(2,1)S(1)} %constant_dynamic-slice_fusion), channel_id=1, source_target_pairs={{0,72},{8,64},{64,8},{72,0},{1,73},{9,65},{65,9},{73,1},{2,74},{10... | collective-permute-start | bytes 983048 | tf_op jit(solution)/shard_map/ppermute | solution.py:324
  28.7 26.6 %collective-permute-done = bf16[40,4096]{1,0:T(8,128)(2,1)S(1)} collective-permute-done((bf16[40,4096]{1,0:T(8,128)(2,1)S(1)}, bf16[40,4096]{1,0:T(8,128)(2,1)S(1)}, u32[]{:S(2)}, u32[]{:S(2)}) %collective-permute-start) | collective-permute-done | bytes 327712 | tf_op jit(solution)/shard_map/ppermute | solution.py:324
  55.3 1.7 fusion
  57.7 1.5 collective-permute-start.3
  59.5 0.8 collective-permute-start.5
  60.3 2.4 collective-permute-start.6
  62.7 2.5 copy-done.10
  65.2 1.5 shard_map.104.rest_0_
  66.7 4.0 %copy-done = bf16[8,1280,512]{2,1,0:T(8,128)(2,1)} copy-done((bf16[8,1280,512]{2,1,0:T(8,128)(2,1)}, bf16[8,1280,512]{2,1,0:T(8,128)(2,1)S(1)}, u32[]{:S(2)}) %copy-start) | copy-done | bytes 10485784
  70.7 9.8 %collective-permute-done.1.rest_4_ = bf16[512,896]{1,0:T(8,128)(2,1)S(1)} collective-permute-done((bf16[512,896]{1,0:T(8,128)(2,1)S(1)}, bf16[512,896]{1,0:T(8,128)(2,1)S(1)}, u32[]{:S(2)}, u32[]{:S(2)}) %collective-permute-start.1) | collective-permute-done | bytes 917536 | tf_op jit(solution)/shard_map/ppermute | solution.py:312
  80.5 1.7 collective-permute-start.2
  82.6 1.1 broadcast_select_fusion
  83.7 0.9 pad.4
  84.6 10.8 %all-gather.2.cloned.1.call-done.t_ref = bf16[640,4096]{1,0:T(8,128)(2,1)} async-done(((bf16[40,4096]{1,0:T(8,128)(2,1)}), bf16[640,4096]{1,0:T(8,128)(2,1)}) %all-gather.2.cloned.1.call-update) | async-done | bytes 5242896 | tf_op jit(solution)/shard_map/all_gather | solution.py:328
  95.5 2.9 %collective-permute-start.7 = (bf16[640,512]{1,0:T(8,128)(2,1)}, bf16[640,512]{1,0:T(8,128)(2,1)S(1)}, u32[]{:S(2)}, u32[]{:S(2)}) collective-permute-start(bf16[640,512]{1,0:T(8,128)(2,1)} %pad.4), channel_id=1, source_target_pairs={{0,64},{64,0},{1,65},{65,1},{2,66},{66,2},{3,67},{67,3},{4,68},{68... | collective-permute-start | bytes 1966088 | tf_op jit(solution)/shard_map/ppermute | solution.py:345
  98.5 4.0 %copy-done.1 = bf16[8,1280,512]{2,1,0:T(8,128)(2,1)S(1)} copy-done((bf16[8,1280,512]{2,1,0:T(8,128)(2,1)S(1)}, bf16[8,1280,512]{2,1,0:T(8,128)(2,1)}, u32[]{:S(2)}) %copy-start.1) | copy-done | bytes 10485784
  102.5 2.5 copy-done.11
  105.0 1.5 shard_map.105.t_ref
  106.4 4.0 %copy-done.2 = bf16[8,1280,512]{2,1,0:T(8,128)(2,1)} copy-done((bf16[8,1280,512]{2,1,0:T(8,128)(2,1)}, bf16[8,1280,512]{2,1,0:T(8,128)(2,1)S(1)}, u32[]{:S(2)}) %copy-start.2) | copy-done | bytes 10485784
  110.5 4.0 %copy-done.3 = bf16[8,1280,512]{2,1,0:T(8,128)(2,1)S(1)} copy-done((bf16[8,1280,512]{2,1,0:T(8,128)(2,1)S(1)}, bf16[8,1280,512]{2,1,0:T(8,128)(2,1)}, u32[]{:S(2)}) %copy-start.3) | copy-done | bytes 10485784
  114.5 10.9 %shard_map.106.acc_ref = f32[1280,896]{1,0:T(8,128)S(1)} custom-call(bf16[8,1280,512]{2,1,0:T(8,128)(2,1)S(1)} %copy-done.3, bf16[512,896]{1,0:T(8,128)(2,1)S(1)} %bitcast.23, bf16[512,896]{1,0:T(8,128)(2,1)S(1)} %bitcast.18, bf16[512,896]{1,0:T(8,128)(2,1)} %collective-permute-done.5.rest_2_, bf16[512,896]{1,0:T(8,128)(2,1)} %collective-permute-done.3.rest_3_, ...), custom_call_target="tpu_custom_call" | custom-call | flops 110100480 | bytes 194560 | tf_op jit(solution)/shard_map/pallas_call | solution.py:141
  125.4 0.8 copy-done.15
  126.3 1.1 copy-done.16
  127.3 6.2 %shard_map.107.d_ref = bf16[1280,896]{1,0:T(8,128)(2,1)S(1)} custom-call(bf16[8,1280,512]{2,1,0:T(8,128)(2,1)S(1)} %copy-done.3, bf16[512,896]{1,0:T(8,128)(2,1)} %collective-permute-done.2.low.rest_6_, bf16[512,896]{1,0:T(8,128)(2,1)} %collective-permute-done.4.high.rest_7_, f32[1280,896]{1,0:T(8,128)S(1)} %shard_map.106.acc_ref, ...), custom_call_target="tpu_custom_call" | custom-call | flops 36700160 | bytes 184320 | tf_op jit(solution)/shard_map/pallas_call | solution.py:169
  133.6 4.4 %shard_map.108 = (bf16[512,896]{1,0:T(8,128)(2,1)}, bf16[512,896]{1,0:T(8,128)(2,1)}) custom-call(bf16[8,1280,512]{2,1,0:T(8,128)(2,1)S(1)} %copy-done.3, bf16[1280,896]{1,0:T(8,128)(2,1)S(1)} %shard_map.107.d_ref), custom_call_target="tpu_custom_call" | custom-call | flops 36700160 | bytes 105472 | tf_op jit(solution)/shard_map/pallas_call | solution.py:215
  138.0 9.7 %shard_map.109 = bf16[2,2,4,640,256]{4,3,2,1,0:T(8,128)(2,1)} custom-call(s32[6]{0:T(128)S(1)} %concatenate.9.where_ref, bf16[1280,896]{1,0:T(8,128)(2,1)S(1)} %shard_map.107.d_ref, bf16[512,896]{1,0:T(8,128)(2,1)S(1)} %bitcast.24, bf16[512,896]{1,0:T(8,128)(2,1)S(1)} %bitcast.19, bf16[512,896]{1,0:T(8,128)(2,1)} %collective-permute-done.5.rest_2_, ...), custom_call_target="tpu_custom_call" | custom-call | flops 73400320 | bytes 221184 | tf_op jit(solution)/shard_map/pallas_call | solution.py:281
  148.2 1.5 collective-permute-start.10
  149.7 4.4 %shard_map.110 = (bf16[512,896]{1,0:T(8,128)(2,1)}, bf16[512,896]{1,0:T(8,128)(2,1)}) custom-call(bf16[8,1280,512]{2,1,0:T(8,128)(2,1)S(1)} %bitcast.14, bf16[1280,896]{1,0:T(8,128)(2,1)S(1)} %shard_map.107.d_ref), custom_call_target="tpu_custom_call" | custom-call | flops 2405181685760 | bytes 105472 | tf_op jit(solution)/shard_map/pallas_call | solution.py:215
  154.1 0.9 collective-permute-start.11
  155.0 2.3 collective-permute-start.12
  157.3 9.4 %shard_map.111 = bf16[2,2,4,640,256]{4,3,2,1,0:T(8,128)(2,1)S(1)} custom-call(s32[6]{0:T(128)S(1)} %concatenate.8.where_ref, bf16[1280,896]{1,0:T(8,128)(2,1)S(1)} %shard_map.107.d_ref, bf16[512,896]{1,0:T(8,128)(2,1)S(1)} %bitcast.25, bf16[512,896]{1,0:T(8,128)(2,1)S(1)} %bitcast.20, bf16[512,896]{1,0:T(8,128)(2,1)} %collective-permute-done.5.rest_2_, ...), custom_call_target="tpu_custom_call" | custom-call | flops 73400320 | bytes 221184 | tf_op jit(solution)/shard_map/pallas_call | solution.py:281
  166.7 2.3 copy-done.5
  169.0 3.9 %collective-permute-done.10.rest_1_ = bf16[512,896]{1,0:T(8,128)(2,1)} collective-permute-done((bf16[512,896]{1,0:T(8,128)(2,1)}, bf16[512,896]{1,0:T(8,128)(2,1)}, u32[]{:S(2)}, u32[]{:S(2)}) %collective-permute-start.10) | collective-permute-done | bytes 917536 | tf_op jit(solution)/shard_map/ppermute | solution.py:315
  172.9 4.2 %copy-done.4 = bf16[8,1280,512]{2,1,0:T(8,128)(2,1)S(1)} copy-done((bf16[8,1280,512]{2,1,0:T(8,128)(2,1)S(1)}, bf16[8,1280,512]{2,1,0:T(8,128)(2,1)}, u32[]{:S(2)}) %copy-start.4) | copy-done | bytes 10485784
  177.1 4.6 %shard_map.112 = (bf16[512,896]{1,0:T(8,128)(2,1)S(1)}, bf16[512,896]{1,0:T(8,128)(2,1)S(1)}) custom-call(bf16[8,1280,512]{2,1,0:T(8,128)(2,1)S(1)} %copy-done.4, bf16[1280,896]{1,0:T(8,128)(2,1)S(1)} %shard_map.107.d_ref, bf16[512,896]{1,0:T(8,128)(2,1)} %collective-permute-done.9.rest_0_, bf16[512,896]{1,0:T(8,128)(2,1)} %collective-permute-done.10.rest_1_), custom_call_target="tpu_custom_call" | custom-call | flops 2405181685760 | bytes 134144 | tf_op jit(solution)/shard_map/pallas_call | solution.py:215
  182.0 1.8 collective-permute-start.14
  183.8 8.8 %collective-permute-done.11.rest_0_ = bf16[512,896]{1,0:T(8,128)(2,1)} collective-permute-done((bf16[512,896]{1,0:T(8,128)(2,1)}, bf16[512,896]{1,0:T(8,128)(2,1)}, u32[]{:S(2)}, u32[]{:S(2)}) %collective-permute-start.11) | collective-permute-done | bytes 917536 | tf_op jit(solution)/shard_map/ppermute | solution.py:315
  192.6 4.6 %shard_map.113.t_ref = f32[1024,896]{1,0:T(8,128)S(1)} custom-call(bf16[8,1280,512]{2,1,0:T(8,128)(2,1)S(1)} %copy-done.4, bf16[1280,896]{1,0:T(8,128)(2,1)S(1)} %shard_map.107.d_ref, bf16[512,896]{1,0:T(8,128)(2,1)} %collective-permute-done.11.rest_0_, bf16[512,896]{1,0:T(8,128)(2,1)} %collective-permute-done.12.rest_1_), custom_call_target="tpu_custom_call" | custom-call | flops 36700160 | bytes 134144 | tf_op jit(solution)/shard_map/pallas_call | solution.py:215
  197.2 12.8 %collective-permute-done.13.l_ref = bf16[512,896]{1,0:T(8,128)(2,1)S(1)} collective-permute-done((bf16[512,896]{1,0:T(8,128)(2,1)S(1)}, bf16[512,896]{1,0:T(8,128)(2,1)S(1)}, u32[]{:S(2)}, u32[]{:S(2)}) %collective-permute-start.13) | collective-permute-done | bytes 917536 | tf_op jit(solution)/shard_map/ppermute | solution.py:312
  210.0 1.5 collective-permute-done.14.h_ref
  212.0 30.6 %all_to_all.10 = bf16[32,32,896]{2,1,0:T(8,128)(2,1)S(1)} all-to-all(bf16[32,32,896]{2,1,0:T(8,128)(2,1)S(1)} %bitcast.26), channel_id=1, replica_groups=mesh['zh'=2,'x'=4,'zl'=2,'y'=4,'c'=2] {'zh','zl','y','c'}, dimensions={0} | all-to-all | bytes 3670016 | tf_op jit(solution)/shard_map/all_to_all | solution.py:318
  242.7 2.1 shard_map.115
  244.7 14.0 %reduce-scatter.2.cloned.1.call-done = bf16[640,256]{1,0:T(8,128)(2,1)} async-done(((bf16[10240,256]{1,0:T(8,128)(2,1)}), bf16[640,256]{1,0:T(8,128)(2,1)}) %reduce-scatter.2.cloned.1.call-update) | async-done | bytes 327696 | tf_op jit(solution)/shard_map/reduce_scatter | solution.py:361
  (67 shorter events, 6.0 us)
Async XLA Ops:
  7.2 1.5 copy-start.13
  8.7 1.5 copy-start.14
  10.2 0.8 copy-start.17
  11.0 0.8 copy-start.18
  11.8 0.7 copy-start.19
  12.5 0.7 copy-start.20
  16.1 39.2 %all-to-all-start = ((bf16[32,32,896]{2,1,0:T(8,128)(2,1)}), bf16[32,32,896]{2,1,0:T(8,128)(2,1)}, u32[]{:S(2)}, u32[]{:S(2)}) async-start(bf16[32,32,896]{2,1,0:T(8,128)(2,1)} %bitcast.6), calls=%async_computation | async-start | bytes 3670016 | tf_op jit(solution)/shard_map/all_to_all | solution.py:318
  24.6 70.9 %all-gather.2.cloned.1.call-start = ((), (), s32[]{:S(2)}) async-start(), calls=%async_computation.3 | async-start | bytes 5570560 | tf_op jit(solution)/shard_map/all_gather | solution.py:328
  25.6 29.7 %collective-permute-start = (bf16[40,4096]{1,0:T(8,128)(2,1)S(1)}, bf16[40,4096]{1,0:T(8,128)(2,1)S(1)}, u32[]{:S(2)}, u32[]{:S(2)}) collective-permute-start(bf16[40,4096]{1,0:T(8,128)(2,1)S(1)} %constant_dynamic-slice_fusion), channel_id=1, source_target_pairs={{0,72},{8,64},{64,8},{72,0},{1,73},{9,65},{65,9},{73,1},{2,74},{10... | collective-permute-start | bytes 983048 | tf_op jit(solution)/shard_map/ppermute | solution.py:324
  55.3 1.8 copy-start.22
  57.0 53.4 %copy-start.6 = (bf16[16,32,896]{2,1,0:T(8,128)(2,1)}, bf16[16,32,896]{2,1,0:T(8,128)(2,1)S(1)}, u32[]{:S(2)}) copy-start(bf16[16,32,896]{2,1,0:T(8,128)(2,1)S(1)} %get-tuple-element.44) | copy-start | bytes 2752516
  57.1 201.7 %reduce-scatter.2.cloned.1.call-start = ((), (), s32[]{:S(2)}) async-start(), calls=%async_computation.4 | async-start | bytes 5570560 | tf_op jit(solution)/shard_map/reduce_scatter | solution.py:361
  57.1 23.3 %collective-permute-start.1 = (bf16[512,896]{1,0:T(8,128)(2,1)S(1)}, bf16[512,896]{1,0:T(8,128)(2,1)S(1)}, u32[]{:S(2)}, u32[]{:S(2)}) collective-permute-start(bf16[512,896]{1,0:T(8,128)(2,1)S(1)} %bitcast.21), channel_id=1, source_target_pairs={{0,16},{16,32},{32,48},{48,0},{1,17},{17,33},{33,49},{49,1},{2,18}... | collective-permute-start | bytes 2752520 | tf_op jit(solution)/shard_map/ppermute | solution.py:312
  57.7 24.6 %collective-permute-start.3 = (bf16[512,896]{1,0:T(8,128)(2,1)S(1)}, bf16[512,896]{1,0:T(8,128)(2,1)}, u32[]{:S(2)}, u32[]{:S(2)}) collective-permute-start(bf16[512,896]{1,0:T(8,128)(2,1)S(1)} %bitcast.16), channel_id=1, source_target_pairs={{0,48},{16,0},{32,16},{48,32},{1,49},{17,1},{33,17},{49,33},{2,50}... | collective-permute-start | bytes 2752520 | tf_op jit(solution)/shard_map/ppermute | solution.py:315
  59.5 51.0 %collective-permute-start.5 = (bf16[512,896]{1,0:T(8,128)(2,1)S(1)}, bf16[512,896]{1,0:T(8,128)(2,1)}, u32[]{:S(2)}, u32[]{:S(2)}) collective-permute-start(bf16[512,896]{1,0:T(8,128)(2,1)S(1)} %bitcast.22), channel_id=1, source_target_pairs={{0,48},{16,0},{32,16},{48,32},{1,49},{17,1},{33,17},{49,33},{2,50}... | collective-permute-start | bytes 2752520 | tf_op jit(solution)/shard_map/ppermute | solution.py:315
  60.3 50.2 %collective-permute-start.6 = (bf16[512,896]{1,0:T(8,128)(2,1)S(1)}, bf16[512,896]{1,0:T(8,128)(2,1)}, u32[]{:S(2)}, u32[]{:S(2)}) collective-permute-start(bf16[512,896]{1,0:T(8,128)(2,1)S(1)} %bitcast.17), channel_id=1, source_target_pairs={{0,16},{16,32},{32,48},{48,0},{1,17},{17,33},{33,49},{49,1},{2,18}... | collective-permute-start | bytes 2752520 | tf_op jit(solution)/shard_map/ppermute | solution.py:312
  62.7 2.5 copy-start.10
  65.2 17.4 %copy-start.21 = (bf16[640,896]{1,0:T(8,128)(2,1)S(1)}, bf16[640,896]{1,0:T(8,128)(2,1)}, u32[]{:S(2)}) copy-start(bf16[640,896]{1,0:T(8,128)(2,1)} %param.9) | copy-start | bytes 3440644
  66.7 4.0 %copy-start = (bf16[8,1280,512]{2,1,0:T(8,128)(2,1)}, bf16[8,1280,512]{2,1,0:T(8,128)(2,1)S(1)}, u32[]{:S(2)}) copy-start(bf16[8,1280,512]{2,1,0:T(8,128)(2,1)S(1)} %shard_map.104.rest_0_) | copy-start | bytes 31457284
  80.5 30.0 %copy-start.8 = (bf16[512,896]{1,0:T(8,128)(2,1)}, bf16[512,896]{1,0:T(8,128)(2,1)S(1)}, u32[]{:S(2)}) copy-start(bf16[512,896]{1,0:T(8,128)(2,1)S(1)} %collective-permute-done.1.rest_4_) | copy-start | bytes 2752516
  80.5 44.9 %collective-permute-start.2 = (bf16[512,896]{1,0:T(8,128)(2,1)S(1)}, bf16[512,896]{1,0:T(8,128)(2,1)}, u32[]{:S(2)}, u32[]{:S(2)}) collective-permute-start(bf16[512,896]{1,0:T(8,128)(2,1)S(1)} %collective-permute-done.1.rest_4_), channel_id=1, source_target_pairs={{0,16},{16,32},{32,48},{48,0},{1,17},{17,33},{33,49},{49,1},{2,18}... | collective-permute-start | bytes 2752520 | tf_op jit(solution)/shard_map/ppermute | solution.py:312
  82.3 43.1 %collective-permute-start.4 = (bf16[512,896]{1,0:T(8,128)(2,1)}, bf16[512,896]{1,0:T(8,128)(2,1)}, u32[]{:S(2)}, u32[]{:S(2)}) collective-permute-start(bf16[512,896]{1,0:T(8,128)(2,1)} %collective-permute-done.3.rest_3_), channel_id=1, source_target_pairs={{0,48},{16,0},{32,16},{48,32},{1,49},{17,1},{33,17},{49,33},{2,50}... | collective-permute-start | bytes 2752520 | tf_op jit(solution)/shard_map/ppermute | solution.py:315
  95.5 29.9 %collective-permute-start.7 = (bf16[640,512]{1,0:T(8,128)(2,1)}, bf16[640,512]{1,0:T(8,128)(2,1)S(1)}, u32[]{:S(2)}, u32[]{:S(2)}) collective-permute-start(bf16[640,512]{1,0:T(8,128)(2,1)} %pad.4), channel_id=1, source_target_pairs={{0,64},{64,0},{1,65},{65,1},{2,66},{66,2},{3,67},{67,3},{4,68},{68... | collective-permute-start | bytes 1966088 | tf_op jit(solution)/shard_map/ppermute | solution.py:345
  98.5 4.0 %copy-start.1 = (bf16[8,1280,512]{2,1,0:T(8,128)(2,1)S(1)}, bf16[8,1280,512]{2,1,0:T(8,128)(2,1)}, u32[]{:S(2)}) copy-start(bf16[8,1280,512]{2,1,0:T(8,128)(2,1)} %copy-done) | copy-start | bytes 31457284
  102.5 2.5 copy-start.11
  105.0 21.3 %copy-start.12 = (bf16[640,448]{1,0:T(8,128)(2,1)S(1)}, bf16[640,448]{1,0:T(8,128)(2,1)}, u32[]{:S(2)}) copy-start(bf16[640,448]{1,0:T(8,128)(2,1)} %get-tuple-element.45.ga_ref) | copy-start | bytes 1720324
  106.4 4.0 %copy-start.2 = (bf16[8,1280,512]{2,1,0:T(8,128)(2,1)}, bf16[8,1280,512]{2,1,0:T(8,128)(2,1)S(1)}, u32[]{:S(2)}) copy-start(bf16[8,1280,512]{2,1,0:T(8,128)(2,1)S(1)} %shard_map.105.t_ref) | copy-start | bytes 31457284
  110.5 4.0 %copy-start.3 = (bf16[8,1280,512]{2,1,0:T(8,128)(2,1)S(1)}, bf16[8,1280,512]{2,1,0:T(8,128)(2,1)}, u32[]{:S(2)}) copy-start(bf16[8,1280,512]{2,1,0:T(8,128)(2,1)} %copy-done.2) | copy-start | bytes 31457284
  125.4 0.8 copy-start.15
  126.3 1.1 copy-start.16
  133.6 4.4 %copy-start.7 = (bf16[16,32,896]{2,1,0:T(8,128)(2,1)S(1)}, bf16[16,32,896]{2,1,0:T(8,128)(2,1)}, u32[]{:S(2)}) copy-start(bf16[16,32,896]{2,1,0:T(8,128)(2,1)} %copy-done.6) | copy-start | bytes 2752516
  133.6 4.4 %copy-start.9 = (bf16[512,896]{1,0:T(8,128)(2,1)S(1)}, bf16[512,896]{1,0:T(8,128)(2,1)}, u32[]{:S(2)}) copy-start(bf16[512,896]{1,0:T(8,128)(2,1)} %copy-done.8) | copy-start | bytes 2752516
  133.6 16.1 %slice-start = ((s8[10485760]{0:T(1024)(128)(4,1)}), s8[4194304]{0:T(1024)(128)(4,1)S(1)}, s32[]{:S(2)}) async-start(s8[10485760]{0:T(1024)(128)(4,1)} %bitcast.13), calls=%async_computation.5 | async-start | bytes 8388608
  133.6 16.1 %slice-start.1 = ((s8[10485760]{0:T(1024)(128)(4,1)}), s8[4194304]{0:T(1024)(128)(4,1)S(1)}, s32[]{:S(2)}) async-start(s8[10485760]{0:T(1024)(128)(4,1)} %bitcast.13), calls=%async_computation.6 | async-start | bytes 8388608
  138.0 11.7 %slice-start.2 = ((s8[10485760]{0:T(1024)(128)(4,1)}), s8[2097152]{0:T(1024)(128)(4,1)S(1)}, s32[]{:S(2)}) async-start(s8[10485760]{0:T(1024)(128)(4,1)} %bitcast.13), calls=%async_computation.7 | async-start | bytes 4194304
  147.7 9.6 %collective-permute-start.8 = (bf16[2,2,4,640,256]{4,3,2,1,0:T(8,128)(2,1)}, bf16[2,2,4,640,256]{4,3,2,1,0:T(8,128)(2,1)}, u32[]{:S(2)}, u32[]{:S(2)}) collective-permute-start(bf16[2,2,4,640,256]{4,3,2,1,0:T(8,128)(2,1)} %shard_map.109), channel_id=1, source_target_pairs={{0,1},{1,0},{2,3},{3,2},{4,5},{5,4},{6,7},{7,6},{8,9},{9,8},{10,11... | collective-permute-start | bytes 15728648 | tf_op jit(solution)/shard_map/ppermute | solution.py:357
  147.7 25.2 %collective-permute-start.9 = (bf16[512,896]{1,0:T(8,128)(2,1)}, bf16[512,896]{1,0:T(8,128)(2,1)}, u32[]{:S(2)}, u32[]{:S(2)}) collective-permute-start(bf16[512,896]{1,0:T(8,128)(2,1)} %get-tuple-element.30), channel_id=1, source_target_pairs={{0,16},{16,32},{32,48},{48,0},{1,17},{17,33},{33,49},{49,1},{2,18}... | collective-permute-start | bytes 2752520 | tf_op jit(solution)/shard_map/ppermute | solution.py:312
  148.2 24.7 %collective-permute-start.10 = (bf16[512,896]{1,0:T(8,128)(2,1)}, bf16[512,896]{1,0:T(8,128)(2,1)}, u32[]{:S(2)}, u32[]{:S(2)}) collective-permute-start(bf16[512,896]{1,0:T(8,128)(2,1)} %get-tuple-element.36), channel_id=1, source_target_pairs={{0,48},{16,0},{32,16},{48,32},{1,49},{17,1},{33,17},{49,33},{2,50}... | collective-permute-start | bytes 2752520 | tf_op jit(solution)/shard_map/ppermute | solution.py:315
  154.1 38.5 %collective-permute-start.11 = (bf16[512,896]{1,0:T(8,128)(2,1)}, bf16[512,896]{1,0:T(8,128)(2,1)}, u32[]{:S(2)}, u32[]{:S(2)}) collective-permute-start(bf16[512,896]{1,0:T(8,128)(2,1)} %get-tuple-element.33), channel_id=1, source_target_pairs={{0,48},{16,0},{32,16},{48,32},{1,49},{17,1},{33,17},{49,33},{2,50}... | collective-permute-start | bytes 2752520 | tf_op jit(solution)/shard_map/ppermute | solution.py:315
  155.0 37.6 %collective-permute-start.12 = (bf16[512,896]{1,0:T(8,128)(2,1)}, bf16[512,896]{1,0:T(8,128)(2,1)}, u32[]{:S(2)}, u32[]{:S(2)}) collective-permute-start(bf16[512,896]{1,0:T(8,128)(2,1)} %get-tuple-element.39), channel_id=1, source_target_pairs={{0,16},{16,32},{32,48},{48,0},{1,17},{17,33},{33,49},{49,1},{2,18}... | collective-permute-start | bytes 2752520 | tf_op jit(solution)/shard_map/ppermute | solution.py:312
  166.7 2.3 copy-start.5
  172.9 4.2 %copy-start.4 = (bf16[8,1280,512]{2,1,0:T(8,128)(2,1)S(1)}, bf16[8,1280,512]{2,1,0:T(8,128)(2,1)}, u32[]{:S(2)}) copy-start(bf16[8,1280,512]{2,1,0:T(8,128)(2,1)} %copy-done.2) | copy-start | bytes 31457284
  181.7 28.3 %collective-permute-start.13 = (bf16[512,896]{1,0:T(8,128)(2,1)S(1)}, bf16[512,896]{1,0:T(8,128)(2,1)S(1)}, u32[]{:S(2)}, u32[]{:S(2)}) collective-permute-start(bf16[512,896]{1,0:T(8,128)(2,1)S(1)} %get-tuple-element.37), channel_id=1, source_target_pairs={{0,16},{16,32},{32,48},{48,0},{1,17},{17,33},{33,49},{49,1},{2,18}... | collective-permute-start | bytes 2752520 | tf_op jit(solution)/shard_map/ppermute | solution.py:312
  182.0 29.4 %collective-permute-start.14 = (bf16[512,896]{1,0:T(8,128)(2,1)S(1)}, bf16[512,896]{1,0:T(8,128)(2,1)S(1)}, u32[]{:S(2)}, u32[]{:S(2)}) collective-permute-start(bf16[512,896]{1,0:T(8,128)(2,1)S(1)} %get-tuple-element.40), channel_id=1, source_target_pairs={{0,48},{16,0},{32,16},{48,32},{1,49},{17,1},{33,17},{49,33},{2,50}... | collective-permute-start | bytes 2752520 | tf_op jit(solution)/shard_map/ppermute | solution.py:315
Sparse Core Ops, SparseCore 0:
  57.2 38.2 all-gather.1
  169.1 89.6 reduce-scatter.1
